TPU v7x, 32 devices: a whole 2x2x4 slice. The times are simulated.
32 devices in a mesh: grp: 2 (over y), mp: 16 (over z, x, core).
Axes of the slice: x: 2, y: 2, z: 4, core: 2. Of those that a mesh axis runs over, the one named last changes fastest.
Arguments:
- query_grad: bfloat16 [64, 8192], P('grp'), parts along dimension 0, may hold values from -0.0625 to 0.0625
- query_input: bfloat16 [64, 8192], P('grp'), parts along dimension 0, may hold values from -6 to 6
- query_ids: int32 [64], P('grp'), parts along dimension 0, may hold values from 0 to 7, never falling along the last dimension, each value on 1 to 8 neighbouring positions
- train_grad: bfloat16 [256, 8192], P('grp'), parts along dimension 0, may hold values from -0.0625 to 0.0625
- train_input: bfloat16 [256, 8192], P('grp'), parts along dimension 0, may hold values from -3 to 3
- train_ids: int32 [256], P('grp'), parts along dimension 0, may hold values from 0 to 15, never falling along the last dimension, each value on 1 to 16 neighbouring positions
- output_basis: bfloat16 [8192, 8192], P(None, 'mp'), may hold values from -0.0625 to 0.0625
- input_basis: bfloat16 [8192, 8192], P(None, 'mp'), may hold values from -0.0625 to 0.0625
- eigenvalues: float32 [8192, 8192], P('mp'), may hold values from 0.05 to 5
Outputs:
- scores: float32 [16, 16], P('grp'), parts along dimension 0
There are 2 independent parts, one for each index of `grp`. A program takes and returns all parts, laid end to end along the dimension named above; an argument that names none is the same for every part. Nothing has to cross between parts.
Inputs may be any that keep to these rules, and one draw needn't show every extreme that they name: `query_ids`: each query is a run of consecutive tokens, 1 to 8 long, one of exactly 8; ids never fall. `train_ids`: each training example is a run of consecutive tokens, 1 to 16 long, one of exactly 16; ids never fall.
All inputs are finite; a program needn't handle non-finite values.
Results may differ from a plain program's by a relative error of at most 0.0049.
Values may be sent and summed in bfloat16 or wider, within the bound.
A program may use at most 256 MiB of HBM per device.

v0:
```python
import math
import jax
import jax.numpy as jnp
from jax import lax
from jax.sharding import PartitionSpec as P

QUERIES = 8
QMOST = 8
TRAIN = 16
damping_shift = 0.25


def rotate(basis, factors):
    return lax.dot_general(
        basis, factors, (((0,), (1,)), ((), ())), preferred_element_type=jnp.float32
    ).astype(jnp.bfloat16)


def query_window(query_ids):
    token_count = query_ids.shape[0]
    labels = jnp.arange(QUERIES, dtype=jnp.int32)
    starts = jnp.sum((query_ids[None, :] < labels[:, None]).astype(jnp.int32), axis=1)
    window = jnp.minimum(
        starts[:, None] + jnp.arange(QMOST, dtype=jnp.int32)[None, :], token_count - 1
    )
    live_slot = jnp.take(query_ids, window) == labels[:, None]
    return (window, live_slot)


def window_rows(columns, window):
    return jnp.transpose(jnp.take(columns, window, axis=1), (1, 2, 0))


def build_precond(left_window, right_cols, eig_cols, window):
    right_window = window_rows(right_cols, window)
    query_count = left_window.shape[0]
    group_size = math.gcd(query_count, 8)
    left_groups = left_window.reshape(
        (query_count // group_size, group_size) + left_window.shape[1:]
    )
    right_groups = right_window.reshape(
        (query_count // group_size, group_size) + right_window.shape[1:]
    )

    def one_group(operands):
        products = jnp.einsum(
            "qms,qma->qsa", operands[0], operands[1], preferred_element_type=jnp.float32
        )
        return (products / (eig_cols[None] + damping_shift)).astype(jnp.bfloat16)

    precond_groups = lax.map(one_group, (left_groups, right_groups))
    return precond_groups.reshape((query_count,) + precond_groups.shape[2:])


def on_device(
    query_grad,
    query_input,
    query_ids,
    train_grad,
    train_input,
    train_ids,
    output_basis,
    input_basis,
    eigenvalues,
):
    query_left = rotate(output_basis, query_grad)
    query_right = rotate(input_basis, query_input)
    train_left = rotate(output_basis, train_grad)
    train_right = rotate(input_basis, train_input)
    window, live_slot = query_window(query_ids)
    left_taken = window_rows(query_left, window)
    left_window = jnp.where(live_slot[:, :, None], left_taken, jnp.zeros((), jnp.bfloat16))
    right_full, train_full = (
        lax.all_gather(query_right, "mp", axis=0, tiled=True),
        lax.all_gather(train_right, "mp", axis=0, tiled=True),
    )
    precond = build_precond(left_window, right_full, eigenvalues, window)
    inner_sum = jnp.einsum("qsa,at->qst", precond, train_full, preferred_element_type=jnp.float32)
    contrib = jnp.einsum(
        "qst,st->qt", inner_sum, train_left.astype(jnp.float32), precision=lax.Precision.HIGHEST
    )
    onehot = (train_ids[:, None] == jnp.arange(TRAIN, dtype=jnp.int32)[None, :]).astype(jnp.float32)
    shares = jnp.dot(contrib, onehot, precision=lax.Precision.HIGHEST)
    return lax.psum(shares, "mp")


def solution(mesh):
    return jax.shard_map(
        on_device,
        mesh=mesh,
        in_specs=(
            P("grp", None),
            P("grp", None),
            P("grp"),
            P("grp", None),
            P("grp", None),
            P("grp"),
            P(None, "mp"),
            P(None, "mp"),
            P("mp", None),
        ),
        out_specs=P("grp", None),
        check_vma=False,
    )
```

profile of v0, /device:TPU:0, one launch (start us, length us, event | category | flops | bytes accessed | tf_op | source)
XLA Modules:
  0.0 167.1 jit_solution(38802841651659386)
XLA Ops:
  6.5 0.0 copy-start
  6.5 0.0 copy-start.1
  6.5 0.0 copy-start.3
  6.5 0.0 all-gather.2.cloned.1.call-start
  6.5 1.6 copy-done
  8.1 6.4 %convolution_convert_fusion = bf16[512,128]{1,0:T(8,128)(2,1)} fusion(bf16[8192,512]{1,0:T(8,128)(2,1)} %param.16, bf16[128,8192]{1,0:T(8,128)(2,1)S(1)} %copy-done), kind=kOutput, calls=%fused_computation.9 | convolution fusion | flops 1073807360 | bytes 10616832 | tf_op jit(solution)/shard_map/dot_general | solution.py:14
  14.5 0.0 all-gather.2.cloned.1.call-update
  14.6 0.0 copy-done.1
  14.6 0.1 convert_reduce_fusion
  14.7 0.1 compare_select_fusion
  14.8 0.1 reshape.101
  14.9 0.8 gather_fusion
  15.6 0.1 reshape.100
  15.7 0.1 iota_compare_fusion.2
  15.8 0.0 copy-done.3
  15.8 4.9 %convolution_convert_fusion.2 = bf16[512,32]{0,1:T(8,128)(2,1)S(1)} fusion(bf16[32,8192]{1,0:T(8,128)(2,1)S(1)} %copy-done.3, bf16[8192,512]{1,0:T(8,128)(2,1)} %param.16), kind=kOutput, calls=%fused_computation.13 | convolution fusion | flops 268451840 | bytes 8945664 | tf_op jit(solution)/shard_map/dot_general | solution.py:14
  20.7 24.6 %all_gather.6 = bf16[8192,32]{0,1:T(8,128)(2,1)S(1)} all-gather(bf16[512,32]{0,1:T(8,128)(2,1)S(1)} %convolution_convert_fusion.2), channel_id=1, replica_groups=mesh['grp'=2,'mp'=16] {'mp'}, dimensions={0}, use_global_device_ids=true | all-gather | bytes 557056 | tf_op jit(solution)/shard_map/all_gather | solution.py:74
  45.4 0.0 copy-start.4
  45.4 2.2 %gather_fusion.2 = bf16[64,8192]{1,0:T(8,128)(2,1)} fusion(bf16[8192,32]{0,1:T(8,128)(2,1)S(1)} %all_gather.6, s32[1024]{0:T(1024)S(1)} %pad_clamp_fusion), kind=kCustom, calls=%fused_computation.2 | custom fusion | bytes 2097408 | tf_op jit(solution)/shard_map/jit(_take)/gather | solution.py:31
  47.6 0.0 copy-done.4
  47.6 4.9 %convolution_convert_fusion.3 = bf16[512,32]{0,1:T(8,128)(2,1)S(1)} fusion(bf16[32,8192]{1,0:T(8,128)(2,1)S(1)} %copy-done.4, bf16[8192,512]{1,0:T(8,128)(2,1)} %param.15), kind=kOutput, calls=%fused_computation.14 | convolution fusion | flops 268451840 | bytes 8945664 | tf_op jit(solution)/shard_map/dot_general | solution.py:14
  52.5 0.7 gather_fusion.1
  53.2 0.0 copy-start.2
  53.2 11.9 %broadcast_add_fusion = f32[512,8192]{1,0:T(8,128)} fusion(f32[512,8192]{1,0:T(8,128)} %param.17), kind=kLoop, calls=%fused_computation.6 | loop fusion | flops 4194304 | bytes 33554432 | tf_op jit(solution)/shard_map/while/body/eval_jaxpr/add | solution.py:49
  65.1 0.0 copy-done.2
  65.1 30.2 %divide_convert_fusion.6 = bf16[8,512,8192]{2,1,0:T(8,128)(2,1)} fusion(f32[512,8192]{1,0:T(8,128)} %broadcast_add_fusion, bf16[64,8192]{1,0:T(8,128)(2,1)S(1)} %copy-done.2, pred[8,8]{1,0:T(8,128)(4,1)S(1)} %get-tuple-element.14, bf16[64,512]{1,0:T(8,128)(2,1)S(1)} %gather_fusion.1, pred[8,8]{1,0:T(8,128)(4,1)S(1)} %get-tuple-element.13), kind=kOutput, calls=%fused_computation.3.clone.clone.clone.clone.1 | convolution fusion | flops 604569600 | bytes 85000320 | tf_op jit(solution)/shard_map/while/body/eval_jaxpr/qms,qma->qsa/dot_general | solution.py:46
  95.3 6.3 %fusion.7 = f32[128,512]{0,1:T(8,128)S(1)} fusion(bf16[8192,512]{1,0:T(8,128)(2,1)} %param.15, bf16[128,8192]{1,0:T(8,128)(2,1)} %param.12), kind=kOutput, calls=%fused_computation.12 | convolution fusion | flops 1073872896 | bytes 10747904 | tf_op jit(solution)/shard_map/dot_general | solution.py:14
  101.7 0.0 copy-start.5
  101.7 0.0 all-gather.2.cloned.1.call-done
  101.7 27.9 %multiply_reduce_fusion = f32[128,8]{0,1:T(8,128)S(1)} fusion(bf16[8192,128]{1,0:T(8,128)(2,1)} %all-gather.2.cloned.1.call-done, f32[128,512]{0,1:T(8,128)S(1)} %fusion.7, bf16[8,512,8192]{2,1,0:T(8,128)(2,1)} %divide_convert_fusion.6), kind=kOutput, calls=%fused_computation.8 | convolution fusion | flops 8590982144 | bytes 69472256 | tf_op jit(solution)/shard_map/qsa,at->qst/dot_general | solution.py:78
  129.6 0.0 copy-done.5
  129.7 0.2 fusion.19
  129.8 30.4 %psum.7 = f32[8,16]{1,0:T(8,128)} all-reduce(f32[8,16]{1,0:T(8,128)S(1)} %fusion.19), channel_id=1, replica_groups=mesh['grp'=2,'mp'=16] {'mp'}, use_global_device_ids=true, to_apply=%region_1.2 | all-reduce | flops 128 | bytes 1024 | tf_op jit(solution)/shard_map/psum | solution.py:84
  (1 shorter events, 0.0 us)
Async XLA Ops:
  6.5 1.6 copy-start
  6.5 8.0 %copy-start.1 = (s32[32]{0:T(128)S(1)}, s32[32]{0:T(128)}, u32[]{:S(2)}) copy-start(s32[32]{0:T(128)} %param.11) | copy-start | bytes 388
  6.5 9.3 %copy-start.3 = (bf16[32,8192]{1,0:T(8,128)(2,1)S(1)}, bf16[32,8192]{1,0:T(8,128)(2,1)}, u32[]{:S(2)}) copy-start(bf16[32,8192]{1,0:T(8,128)(2,1)} %param.10) | copy-start | bytes 1572868
  6.5 95.2 %all-gather.2.cloned.1.call-start = ((), (), s32[]{:S(2)}) async-start(), calls=%async_computation | async-start | bytes 2228224 | tf_op jit(solution)/shard_map/all_gather | solution.py:75
  45.4 2.2 %copy-start.4 = (bf16[32,8192]{1,0:T(8,128)(2,1)S(1)}, bf16[32,8192]{1,0:T(8,128)(2,1)}, u32[]{:S(2)}) copy-start(bf16[32,8192]{1,0:T(8,128)(2,1)} %param.9) | copy-start | bytes 1572868
  53.2 11.9 %copy-start.2 = (bf16[64,8192]{1,0:T(8,128)(2,1)S(1)}, bf16[64,8192]{1,0:T(8,128)(2,1)}, u32[]{:S(2)}) copy-start(bf16[64,8192]{1,0:T(8,128)(2,1)} %gather_fusion.2) | copy-start | bytes 3145732
  101.7 28.0 %copy-start.5 = (s32[128]{0:T(128)S(1)}, s32[128]{0:T(128)}, u32[]{:S(2)}) copy-start(s32[128]{0:T(128)} %param.14) | copy-start | bytes 1540
Sparse Core Ops, SparseCore 0:
  14.7 44.4 all-gather.1
where the time goes:
time: 167 us
  matrix products  81 us (49%)
  blocking collectives  55.1 us (33%)
  between operations  13.5 us (8%)
  other arithmetic  12.1 us (7%)
  local copies, waits for them, and re-layouts  5.45 us (3%)
    psum x1, blocking collectives, on_device(): return lax.psum(shares, 'mp')  30.4 us
    dot_general x1, matrix products, one_group(): jnp.einsum('qms,qma->qsa', operands[0], operands[1], preferred_element_ty...  30.2 us
    dot_general x1, matrix products, on_device(): jnp.einsum('qsa,at->qst', precond, train_full, preferred_element_type=jnp...  27.9 us
    all_gather x1, blocking collectives, on_device(): lax.all_gather(query_right, 'mp', axis=0, tiled=True)  24.6 us
    dot_general x4, matrix products, rotate(): lax.dot_general(basis, factors, (((0,), (1,)), ((), ())), preferred_eleme...  22.6 us
    add x1, other arithmetic, one_group(): return (products / (eig_cols[None] + damping_shift)).astype(jnp.bfloat16)  11.9 us
  transfers between devices with their start and end apart: 1, of which 0 were waited for; matrix products, arithmetic and copies ran while one was open for 37% of the time, Pallas kernels for 0%

commit v1 on v0

--- a/solution.py
+++ b/solution.py
@@ -81,7 +81,7 @@
     )
     onehot = (train_ids[:, None] == jnp.arange(TRAIN, dtype=jnp.int32)[None, :]).astype(jnp.float32)
     shares = jnp.dot(contrib, onehot, precision=lax.Precision.HIGHEST)
-    return lax.psum(shares, "mp")
+    return jnp.sum(lax.all_gather(shares, "mp"), axis=0)
 
 
 def solution(mesh):

time: 167 us -> 155 us (0.928)
  blocking collectives: 55.1 us -> 42.3 us
    psum x1 -> x0, blocking collectives: 30.4 us -> none  [on_device(): return lax.psum(shares, 'mp')]
    all_gather x0 -> x1, blocking collectives: none -> 17.6 us  [on_device(): return jnp.sum(lax.all_gather(shares, 'mp'), axis=0)]
  transfers between devices with their start and end apart: 1 -> 1, of which waited for: 0 -> 0; matrix products, arithmetic and copies ran while one was open for 37% -> 40% of each run, Pallas kernels for 0% -> 0%
where the time goes in v1:
time: 155 us
  matrix products  81 us (52%)
  blocking collectives  42.3 us (27%)
  between operations  13.5 us (9%)
  other arithmetic  12.8 us (8%)
  local copies, waits for them, and re-layouts  5.45 us (4%)
    dot_general x1, matrix products, one_group(): jnp.einsum('qms,qma->qsa', operands[0], operands[1], preferred_element_ty...  30.2 us
    dot_general x1, matrix products, on_device(): jnp.einsum('qsa,at->qst', precond, train_full, preferred_element_type=jnp...  27.9 us
    all_gather x1, blocking collectives, on_device(): lax.all_gather(query_right, 'mp', axis=0, tiled=True)  24.6 us
    dot_general x4, matrix products, rotate(): lax.dot_general(basis, factors, (((0,), (1,)), ((), ())), preferred_eleme...  22.6 us
    all_gather x1, blocking collectives, on_device(): return jnp.sum(lax.all_gather(shares, 'mp'), axis=0)  17.6 us
    add x1, other arithmetic, one_group(): return (products / (eig_cols[None] + damping_shift)).astype(jnp.bfloat16)  11.9 us
  transfers between devices with their start and end apart: 1, of which 0 were waited for; matrix products, arithmetic and copies ran while one was open for 40% of the time, Pallas kernels for 0%

profile of v1, /device:TPU:0, one launch (start us, length us, event | category | flops | bytes accessed | tf_op | source)
XLA Modules:
  0.0 154.9 jit_solution(14958794453660524945)
XLA Ops:
  6.5 0.0 copy-start
  6.5 0.0 copy-start.1
  6.5 0.0 copy-start.3
  6.5 0.0 all-gather.3.cloned.1.call-start
  6.5 1.6 %copy-done = bf16[128,8192]{1,0:T(8,128)(2,1)S(1)} copy-done((bf16[128,8192]{1,0:T(8,128)(2,1)S(1)}, bf16[128,8192]{1,0:T(8,128)(2,1)}, u32[]{:S(2)}) %copy-start) | copy-done | bytes 2097176
  8.1 6.4 %convolution_convert_fusion = bf16[512,128]{1,0:T(8,128)(2,1)} fusion(bf16[8192,512]{1,0:T(8,128)(2,1)} %param.16, bf16[128,8192]{1,0:T(8,128)(2,1)S(1)} %copy-done), kind=kOutput, calls=%fused_computation.9 | convolution fusion | flops 1073807360 | bytes 10616832 | tf_op jit(solution)/shard_map/dot_general | solution.py:14
  14.5 0.0 all-gather.3.cloned.1.call-update
  14.6 0.0 copy-done.1
  14.6 0.1 convert_reduce_fusion
  14.7 0.1 compare_select_fusion
  14.8 0.1 reshape.101
  14.9 0.8 gather_fusion
  15.6 0.1 reshape.100
  15.7 0.1 iota_compare_fusion.2
  15.8 0.0 copy-done.3
  15.8 4.9 %convolution_convert_fusion.2 = bf16[512,32]{0,1:T(8,128)(2,1)S(1)} fusion(bf16[32,8192]{1,0:T(8,128)(2,1)S(1)} %copy-done.3, bf16[8192,512]{1,0:T(8,128)(2,1)} %param.16), kind=kOutput, calls=%fused_computation.13 | convolution fusion | flops 268451840 | bytes 8945664 | tf_op jit(solution)/shard_map/dot_general | solution.py:14
  20.7 24.6 %all_gather.12 = bf16[8192,32]{0,1:T(8,128)(2,1)S(1)} all-gather(bf16[512,32]{0,1:T(8,128)(2,1)S(1)} %convolution_convert_fusion.2), channel_id=1, replica_groups=mesh['grp'=2,'mp'=16] {'mp'}, dimensions={0}, use_global_device_ids=true | all-gather | bytes 557056 | tf_op jit(solution)/shard_map/all_gather | solution.py:74
  45.4 0.0 copy-start.4
  45.4 2.2 %gather_fusion.2 = bf16[64,8192]{1,0:T(8,128)(2,1)} fusion(bf16[8192,32]{0,1:T(8,128)(2,1)S(1)} %all_gather.12, s32[1024]{0:T(1024)S(1)} %pad_clamp_fusion), kind=kCustom, calls=%fused_computation.2 | custom fusion | bytes 2097408 | tf_op jit(solution)/shard_map/jit(_take)/gather | solution.py:31
  47.6 0.0 copy-done.4
  47.6 4.9 %convolution_convert_fusion.3 = bf16[512,32]{0,1:T(8,128)(2,1)S(1)} fusion(bf16[32,8192]{1,0:T(8,128)(2,1)S(1)} %copy-done.4, bf16[8192,512]{1,0:T(8,128)(2,1)} %param.15), kind=kOutput, calls=%fused_computation.14 | convolution fusion | flops 268451840 | bytes 8945664 | tf_op jit(solution)/shard_map/dot_general | solution.py:14
  52.5 0.7 gather_fusion.1
  53.2 0.0 copy-start.2
  53.2 11.9 %broadcast_add_fusion = f32[512,8192]{1,0:T(8,128)} fusion(f32[512,8192]{1,0:T(8,128)} %param.17), kind=kLoop, calls=%fused_computation.6 | loop fusion | flops 4194304 | bytes 33554432 | tf_op jit(solution)/shard_map/while/body/eval_jaxpr/add | solution.py:49
  65.1 0.0 copy-done.2
  65.1 30.2 %divide_convert_fusion.6 = bf16[8,512,8192]{2,1,0:T(8,128)(2,1)} fusion(f32[512,8192]{1,0:T(8,128)} %broadcast_add_fusion, bf16[64,8192]{1,0:T(8,128)(2,1)S(1)} %copy-done.2, pred[8,8]{1,0:T(8,128)(4,1)S(1)} %get-tuple-element.14, bf16[64,512]{1,0:T(8,128)(2,1)S(1)} %gather_fusion.1, pred[8,8]{1,0:T(8,128)(4,1)S(1)} %get-tuple-element.13), kind=kOutput, calls=%fused_computation.3.clone.clone.clone.clone.1 | convolution fusion | flops 604569600 | bytes 85000320 | tf_op jit(solution)/shard_map/while/body/eval_jaxpr/qms,qma->qsa/dot_general | solution.py:46
  95.3 6.3 %fusion.7 = f32[128,512]{0,1:T(8,128)S(1)} fusion(bf16[8192,512]{1,0:T(8,128)(2,1)} %param.15, bf16[128,8192]{1,0:T(8,128)(2,1)} %param.12), kind=kOutput, calls=%fused_computation.12 | convolution fusion | flops 1073872896 | bytes 10747904 | tf_op jit(solution)/shard_map/dot_general | solution.py:14
  101.7 0.0 copy-start.5
  101.7 0.0 all-gather.3.cloned.1.call-done
  101.7 27.9 %multiply_reduce_fusion = f32[128,8]{0,1:T(8,128)S(1)} fusion(bf16[8192,128]{1,0:T(8,128)(2,1)} %all-gather.3.cloned.1.call-done, f32[128,512]{0,1:T(8,128)S(1)} %fusion.7, bf16[8,512,8192]{2,1,0:T(8,128)(2,1)} %divide_convert_fusion.6), kind=kOutput, calls=%fused_computation.8 | convolution fusion | flops 8590982144 | bytes 69472256 | tf_op jit(solution)/shard_map/qsa,at->qst/dot_general | solution.py:78
  129.6 0.0 copy-done.5
  129.7 0.2 fusion.19
  129.8 17.6 %all-gather = f32[128,16]{1,0:T(8,128)S(1)} all-gather(f32[8,16]{1,0:T(8,128)S(1)} %fusion.19), channel_id=2, replica_groups=mesh['grp'=2,'mp'=16] {'mp'}, dimensions={0}, use_global_device_ids=true | all-gather | bytes 8704 | tf_op jit(solution)/shard_map/all_gather | solution.py:84
  147.5 0.6 bitcast_reduce_fusion
  (1 shorter events, 0.0 us)
Async XLA Ops:
  6.5 1.6 %copy-start = (bf16[128,8192]{1,0:T(8,128)(2,1)S(1)}, bf16[128,8192]{1,0:T(8,128)(2,1)}, u32[]{:S(2)}) copy-start(bf16[128,8192]{1,0:T(8,128)(2,1)} %param.13) | copy-start | bytes 6291460
  6.5 8.0 %copy-start.1 = (s32[32]{0:T(128)S(1)}, s32[32]{0:T(128)}, u32[]{:S(2)}) copy-start(s32[32]{0:T(128)} %param.11) | copy-start | bytes 388
  6.5 9.3 %copy-start.3 = (bf16[32,8192]{1,0:T(8,128)(2,1)S(1)}, bf16[32,8192]{1,0:T(8,128)(2,1)}, u32[]{:S(2)}) copy-start(bf16[32,8192]{1,0:T(8,128)(2,1)} %param.10) | copy-start | bytes 1572868
  6.5 95.2 %all-gather.3.cloned.1.call-start = ((), (), s32[]{:S(2)}) async-start(), calls=%async_computation | async-start | bytes 2228224 | tf_op jit(solution)/shard_map/all_gather | solution.py:75
  45.4 2.2 %copy-start.4 = (bf16[32,8192]{1,0:T(8,128)(2,1)S(1)}, bf16[32,8192]{1,0:T(8,128)(2,1)}, u32[]{:S(2)}) copy-start(bf16[32,8192]{1,0:T(8,128)(2,1)} %param.9) | copy-start | bytes 1572868
  53.2 11.9 %copy-start.2 = (bf16[64,8192]{1,0:T(8,128)(2,1)S(1)}, bf16[64,8192]{1,0:T(8,128)(2,1)}, u32[]{:S(2)}) copy-start(bf16[64,8192]{1,0:T(8,128)(2,1)} %gather_fusion.2) | copy-start | bytes 3145732
  101.7 28.0 %copy-start.5 = (s32[128]{0:T(128)S(1)}, s32[128]{0:T(128)}, u32[]{:S(2)}) copy-start(s32[128]{0:T(128)} %param.14) | copy-start | bytes 1540
Sparse Core Ops, SparseCore 0:
  14.7 44.4 all-gather.2
